TPU v7x, 512 devices: a whole 4x4x16 slice. The times are simulated.
512 devices in a mesh: grp: 2 (over x_hi), seq: 32 (over x_lo, z), head: 8 (over y, core).
Axes of the slice: x: 4 (x_hi: 2, x_lo: 2; x = x_hi * 2 + x_lo), y: 4, z: 16, core: 2. Of those that a mesh axis runs over, the one named last changes fastest.
Arguments:
- features: bfloat16 [2, 32, 16, 32, 512], P('grp', 'seq', 'head'), may hold values from -6 to 6
- conv_weight: bfloat16 [3, 3, 3, 512, 16], replicated, may hold values from -0.0546875 to 0.0546875
- conv_bias: float32 [16], replicated, may hold values from -3 to 3
- token_order: int32 [4096], P('seq'), may hold values from 0 to 4095, each once
- embed_weight: bfloat16 [64, 3072], replicated, may hold values from -0.75 to 0.75
- norm_gain: float32 [3072], replicated, may hold values from 0.1 to 1.9
- qkv_weight: bfloat16 [3072, 3, 2048], P('seq', None, 'head'), may hold values from -0.109375 to 0.109375
- grad_out: bfloat16 [2, 4096, 2048], P('grp', 'seq', 'head'), may hold values from -6 to 6
Outputs:
- attended: bfloat16 [2, 4096, 2048], P('grp', 'seq', 'head')
- embed_grad: float32 [64, 3072], P(None, 'head')
All inputs are finite; a program needn't handle non-finite values.
Results may differ from a plain program's by a relative error of at most 0.0052.
Values may be sent and summed in bfloat16 or wider, within the bound.
No kernel may reach another device: no remote copies, remote signals or barrier semaphores. Data moves between devices by JAX's collectives and lax.ppermute only.
A program may use at most 64 MiB of HBM per device.

v0:
```python
import jax
import jax.numpy as jnp
from jax import lax
from jax.sharding import Mesh
from jax.sharding import PartitionSpec as P

D = 3072
HEAD_DIM = 64
SEQ = ("seq_0", "seq_1")
HEAD = ("head_0", "head_1")
GRP_SEQ = ("grp", "seq_0", "seq_1")


def shifted(value, axis, steps):
    count = lax.axis_size(axis)
    leading, last = (max(0, -steps), min(count, count - steps))
    return lax.ppermute(value, axis, [(source, source + steps) for source in range(leading, last)])


def extended(block, sides, width):
    for axis, dim in sides:
        count = lax.axis_size(axis)
        forward = [(i, i + 1) for i in range(count - 1)]
        backward = [(target, source) for source, target in forward]
        low = lax.ppermute(
            lax.slice_in_dim(block, block.shape[dim] - width, None, axis=dim), axis, forward
        )
        high = lax.ppermute(lax.slice_in_dim(block, 0, width, axis=dim), axis, backward)
        block = jnp.concatenate([low, block, high], axis=dim)
    return block


def from_everyone(array, axis):
    copies = jnp.broadcast_to(array, (lax.axis_size(axis), *array.shape))
    return lax.all_to_all(copies, axis, split_axis=0, concat_axis=0, tiled=True)


def joined_along(blocks, dim):
    lengths = list(blocks.shape[1:])
    lengths[dim] *= blocks.shape[0]
    return jnp.moveaxis(blocks, 0, dim).reshape(lengths)


def gather_axes(array, axes, dim):
    far, near = axes
    leading = from_everyone(array, far)
    blocks = jnp.swapaxes(from_everyone(leading, near), 0, 1)
    return joined_along(blocks.reshape(-1, *array.shape), dim)


def side_by_side(arrays, axis, dim, along):
    widths = [a.shape[along] for a in arrays]
    both = jnp.concatenate(arrays, axis=along)
    result = lax.all_gather(both, axis, axis=dim, tiled=True)
    return tuple(jnp.split(result, [sum(widths[:k]) for k in range(1, len(widths))], axis=along))


def split_up(array, dim, devices):
    before, after = (array.shape[:dim], array.shape[dim + 1 :])
    return jnp.moveaxis(array.reshape(*before, devices, -1, *after), dim, 0)


def sent_and_summed(array, axis, dim):
    devices = lax.axis_size(axis)
    blocks = lax.all_to_all(split_up(array, dim, devices), axis, 0, 0, tiled=True)
    return jnp.sum(blocks.astype(jnp.float32), axis=0)


def taken_together(array, axis):
    everything = from_everyone(array, axis)
    return jnp.sum(everything, axis=0)


def sent_and_summed_2(array, axis, dim):
    blocks = split_up(array, dim, lax.axis_size(axis))
    arrived = lax.all_to_all(blocks, axis, split_axis=0, concat_axis=0, tiled=True)
    return arrived.sum(axis=0)


def padded_to(lines, devices):
    spare = -lines.shape[0] % devices
    if not spare:
        return lines
    return jnp.concatenate([lines, jnp.zeros((spare, *lines.shape[1:]), lines.dtype)])


def gather_directly(array, axis, dim):
    return joined_along(from_everyone(array, axis), dim)


def nested_sum(array, axes):
    lines = array.reshape(-1, array.shape[-1])
    own = sent_and_summed_2(padded_to(lines, lax.axis_size(axes)), axes, 0)
    whole = gather_directly(own, axes, 0)
    return whole[: len(lines)].reshape(array.shape)


def patchify(latent):
    frames, rows, columns, channels = latent.shape
    blocks = latent.reshape(frames, rows // 2, 2, columns // 2, 2, channels)
    blocks = jnp.transpose(blocks, (0, 1, 3, 2, 4, 5))
    return blocks.reshape(frames * (rows // 2) * (columns // 2), 4 * channels)


def encode_tile(tile, conv_weight, conv_bias):
    frames, rows, columns, channels = tile.shape
    hops = (frames + 1) // frames
    earlier = []
    for hop in range(hops, 0, -1):
        earlier.append(shifted(tile, SEQ, hop))
    stacked = jnp.concatenate(earlier + [tile], axis=0)
    padded = extended(stacked, ((HEAD, 1),), 1)
    padded = jnp.pad(padded, ((0, 0), (0, 0), (1, 1), (0, 0)))
    total = jnp.zeros((frames * rows * columns, conv_weight.shape[-1]), jnp.float32) + conv_bias
    for a in range(3):
        for b in range(3):
            for e in range(3):
                piece = padded[a : a + frames, b : b + rows, e : e + columns].reshape(-1, channels)
                total = total + jnp.dot(
                    piece, conv_weight[a, b, e], preferred_element_type=jnp.float32
                )
    return total.astype(jnp.bfloat16).reshape(frames, rows, columns, conv_weight.shape[-1])


def head_major(matrix, head_local):
    count = matrix.shape[0]
    return jnp.transpose(matrix.reshape(count, head_local, HEAD_DIM), (1, 0, 2))


def row_major(stacked):
    heads_here, count, size = stacked.shape
    return jnp.transpose(stacked, (1, 0, 2)).reshape(count, heads_here * size)


def head_forward(operands):
    query, keys, values, cotan = operands
    factor = HEAD_DIM ** (-0.5)
    scores = jnp.dot(query, keys.T, preferred_element_type=jnp.float32) * factor
    top = jnp.max(scores, axis=-1, keepdims=True)
    lse = top + jnp.log(jnp.sum(jnp.exp(scores - top), axis=-1, keepdims=True))
    probs = jnp.exp(scores - lse)
    probs_low = probs.astype(jnp.bfloat16)
    output = jnp.dot(probs_low, values, preferred_element_type=jnp.float32).astype(jnp.bfloat16)
    delta = jnp.sum(cotan.astype(jnp.float32) * output.astype(jnp.float32), axis=-1, keepdims=True)
    dprob = jnp.dot(cotan, values.T, preferred_element_type=jnp.float32)
    dscore = (probs * (dprob - delta)).astype(jnp.bfloat16)
    grad_q = jnp.dot(dscore, keys, preferred_element_type=jnp.float32) * factor
    return (output, lse[:, 0], delta[:, 0], grad_q)


def head_backward(operands):
    query, cotan, lse_piece, delta_piece, own_keys, own_values = operands
    factor = HEAD_DIM ** (-0.5)
    scores = jnp.dot(query, own_keys.T, preferred_element_type=jnp.float32) * factor
    probs = jnp.exp(scores - lse_piece[:, None])
    value_add = jnp.dot(probs.astype(jnp.bfloat16).T, cotan, preferred_element_type=jnp.float32)
    dprob = jnp.dot(cotan, own_values.T, preferred_element_type=jnp.float32)
    dscore = (probs * (dprob - delta_piece[:, None])).astype(jnp.bfloat16)
    key_add = jnp.dot(dscore.T, query, preferred_element_type=jnp.float32)
    return (key_add, value_add)


def per_device(
    features, conv_weight, conv_bias, token_order, embed_weight, norm_gain, qkv_weight, grad_out
):
    tile = encode_tile(features[0], conv_weight, conv_bias)
    frames, rows, columns, channels = tile.shape
    every = gather_axes(tile[None], (("seq_0", "seq_1"), ("head_0", "head_1")), 0)
    seq_count = lax.axis_size(SEQ)
    head_count = lax.axis_size(HEAD)
    every = every.reshape(seq_count, head_count, frames, rows, columns, channels)
    every = jnp.transpose(every, (0, 2, 1, 3, 4, 5))
    whole = every.reshape(seq_count * frames, head_count * rows, columns, channels)
    patches = patchify(whole)
    tokens = jnp.take(patches, token_order, axis=0)
    local_rows = tokens.shape[0]
    mixed = jnp.dot(tokens, embed_weight, preferred_element_type=jnp.float32)
    inverse = lax.rsqrt(jnp.mean(mixed * mixed, axis=-1, keepdims=True) + 1e-06)
    normal = mixed * inverse
    hidden = (normal * norm_gain).astype(jnp.bfloat16)
    full_weight = lax.all_gather(qkv_weight, SEQ, axis=0, tiled=True)
    local_width = full_weight.shape[2]
    head_local = local_width // HEAD_DIM
    flat_weight = full_weight.reshape(D, 3 * local_width)
    proj = jnp.dot(hidden, flat_weight, preferred_element_type=jnp.float32).astype(jnp.bfloat16)
    proj = proj.reshape(local_rows, 3, local_width)
    query = proj[:, 0]
    keys_all, values_all = side_by_side((proj[:, 1], proj[:, 2]), SEQ, 0, 1)
    cotan = grad_out[0]
    output_h, lse_h, delta_h, grad_q_h = lax.map(
        head_forward,
        (
            head_major(query, head_local),
            head_major(keys_all, head_local),
            head_major(values_all, head_local),
            head_major(cotan, head_local),
        ),
    )
    output = row_major(output_h)
    grad_q = row_major(grad_q_h)
    lse_all, delta_all = side_by_side((jnp.transpose(lse_h), jnp.transpose(delta_h)), SEQ, 0, 1)
    own_keys = head_major(proj[:, 1], head_local)
    own_values = head_major(proj[:, 2], head_local)
    query_piece, cotan_piece = side_by_side((query, cotan), SEQ, 0, 1)
    lse_piece = jnp.transpose(lse_all)
    delta_piece = jnp.transpose(delta_all)
    key_add, value_add = lax.map(
        head_backward,
        (
            head_major(query_piece, head_local),
            head_major(cotan_piece, head_local),
            lse_piece,
            delta_piece,
            own_keys,
            own_values,
        ),
    )
    grad_k = row_major(key_add * HEAD_DIM ** (-0.5))
    grad_v = row_major(value_add)
    grads = (
        jnp.stack([grad_q, grad_k, grad_v], axis=1)
        .reshape(local_rows, 3 * local_width)
        .astype(jnp.bfloat16)
    )
    back_part = lax.dot_general(
        grads, flat_weight, (((1,), (1,)), ((), ())), preferred_element_type=jnp.float32
    )
    head_count_d = lax.axis_size(HEAD)
    width_dev = D // head_count_d
    start_col = lax.axis_index(HEAD) * width_dev
    normal_own = lax.dynamic_slice_in_dim(normal, start_col, width_dev, 1)
    gain_own = lax.dynamic_slice_in_dim(norm_gain, start_col, width_dev, 0)
    back_own = sent_and_summed(back_part.astype(jnp.bfloat16), HEAD, 1)
    scaled_own = back_own * gain_own
    inner_part = jnp.sum(scaled_own * normal_own, axis=-1, keepdims=True)
    inner = taken_together(inner_part, HEAD) / D
    dmixed_own = inverse * (scaled_own - normal_own * inner)
    embed_part = jnp.dot(
        tokens.astype(jnp.float32).T,
        dmixed_own,
        preferred_element_type=jnp.float32,
        precision=lax.Precision.HIGHEST,
    )
    embed_grad = nested_sum(embed_part, GRP_SEQ)
    attended = output.reshape(1, local_rows, local_width)
    return (attended, embed_grad)


def solution(mesh):
    torus = Mesh(
        mesh.devices.reshape(mesh.shape["grp"], 2, 16, 4, 2),
        ("grp", "seq_0", "seq_1", "head_0", "head_1"),
    )
    return jax.shard_map(
        per_device,
        mesh=torus,
        in_specs=(
            P("grp", SEQ, HEAD, None, None),
            P(),
            P(),
            P(SEQ),
            P(),
            P(),
            P(SEQ, None, HEAD),
            P("grp", SEQ, HEAD),
        ),
        out_specs=(P("grp", SEQ, HEAD), P(None, HEAD)),
        check_vma=False,
    )
```

profile of v0, /device:TPU:2, one launch (start us, length us, event | category | flops | bytes accessed | tf_op | source)
XLA Modules:
  0.0 568.6 jit_solution(3382214532136301586)
XLA Ops:
  7.2 5.3 collective-permute-start
  16.4 5.2 collective-permute-done
  36.5 23.9 %all_to_all.33 = bf16[32,2,512]{2,1,0:T(2,128)(2,1)S(1)} all-to-all(bf16[32,2,512]{2,1,0:T(2,128)(2,1)S(1)} %reshape.224), channel_id=1, replica_groups=mesh['grp'=2,'seq_0'=2,'seq_1'=16,'head_0'=4,'head_1'=2] {'seq_0','seq_1'}, dimensions={0} | all-to-all | bytes 131072 | tf_op jit(solution)/shard_map/all_to_all | solution.py:35
  64.2 7.5 %all-to-all-start.1 = ((bf16[8,2,16384]{2,1,0:T(2,128)(2,1)}), bf16[8,2,16384]{2,1,0:T(2,128)(2,1)S(1)}, u32[]{:S(2)}, u32[]{:S(2)}) async-start(bf16[8,2,16384]{2,1,0:T(2,128)(2,1)} %reshape.226), calls=%async_computation.1 | async-start | bytes 1048576 | tf_op jit(solution)/shard_map/all_to_all | solution.py:35
  71.7 10.3 %all-to-all-done.1 = bf16[8,2,16384]{2,1,0:T(2,128)(2,1)S(1)} async-done(((bf16[8,2,16384]{2,1,0:T(2,128)(2,1)}), bf16[8,2,16384]{2,1,0:T(2,128)(2,1)S(1)}, u32[]{:S(2)}, u32[]{:S(2)}) %all-to-all-start.1) | async-done | bytes 524320 | tf_op jit(solution)/shard_map/all_to_all | solution.py:35
  83.0 9.7 %copy.86 = bf16[32,8,16,2,2,16]{5,4,3,2,1,0:T(2,128)(2,1)} copy(bf16[32,8,16,2,2,16]{0,5,4,2,3,1:T(8,128)(2,1)S(1)} %bitcast.364) | data formatting | bytes 1048576 | tf_op jit(solution)/shard_map/reshape | solution.py:102
  92.7 8.0 %reshape.223 = bf16[4096,64]{1,0:T(8,128)(2,1)S(1)} reshape(bf16[32,8,16,2,2,16]{5,4,3,2,1,0:T(2,128)(2,1)} %copy.86) | data formatting | bytes 1048576 | tf_op jit(solution)/shard_map/reshape | solution.py:102
  102.1 64.1 %all-gather.4.cloned.1.call-done = bf16[3072,3,256]{2,0,1:T(8,128)(2,1)} async-done(((bf16[96,3,256]{2,0,1:T(8,128)(2,1)}), bf16[3072,3,256]{2,0,1:T(8,128)(2,1)}) %all-gather.4.cloned.1.call-update) | async-done | bytes 4718608 | tf_op jit(solution)/shard_map/all_gather | solution.py:181
  166.2 6.7 %copy.67 = bf16[3072,3,256]{0,2,1:T(8,128)(2,1)} copy(bf16[3072,3,256]{2,0,1:T(8,128)(2,1)} %all-gather.4.cloned.1.call-done) | data formatting | bytes 9437184 | tf_op jit(solution)/shard_map/all_gather | solution.py:181
  172.9 4.0 convolution_convert_fusion.1
  179.0 135.7 %all-gather.6.cloned.1.call-done = bf16[4096,512]{0,1:T(8,128)(2,1)} async-done(((bf16[128,512]{0,1:T(8,128)(2,1)}), bf16[4096,512]{0,1:T(8,128)(2,1)}) %all-gather.6.cloned.1.call-update) | async-done | bytes 4194320 | tf_op jit(solution)/shard_map/all_gather | solution.py:54
  314.7 4.6 fusion.160
  319.4 23.7 %while.30 = (s32[]{:T(128)}, bf16[4,128,64]{1,2,0:T(8,128)(2,1)S(1)}, f32[4,128]{1,0:T(4,128)S(1)}, f32[4,128]{1,0:T(4,128)S(1)}, bf16[4,128,64]{1,2,0:T(8,128)(...) while((s32[]{:T(128)}, ...), condition=%wide.region_5.6_spmd.clone, body=%wide.region_1.0_spmd.sunk.clone | while | flops 273727232 | bytes 10628201 | solution.py:190
  343.1 61.5 %all_gather.15 = f32[4096,8]{0,1:T(8,128)S(1)} all-gather(f32[128,8]{0,1:T(8,128)S(1)} %pad_maximum_fusion.13), channel_id=1, replica_groups=mesh['grp'=2,'seq_0'=2,'seq_1'=16,'head_0'=4,'head_1'=2] {'seq_0','seq_1'}, dimensions={0}, use_global_device_ids=true | all-gather | bytes 135168 | tf_op jit(solution)/shard_map/all_gather | solution.py:54
  404.6 50.6 %all-gather.8.cloned.1.call-done = bf16[4096,512]{0,1:T(8,128)(2,1)} async-done(((bf16[128,512]{0,1:T(8,128)(2,1)}), bf16[4096,512]{0,1:T(8,128)(2,1)}) %all-gather.8.cloned.1.call-update) | async-done | bytes 4194320 | tf_op jit(solution)/shard_map/all_gather | solution.py:54
  455.3 4.8 fusion.159
  460.0 22.7 %while.31 = (s32[]{:T(128)}, f32[4,128,64]{1,2,0:T(8,128)S(1)}, bf16[4,128,64]{1,2,0:T(8,128)(2,1)S(1)}, bf16[4,4096,64]{1,2,0:T(8,128)(2,1)}, bf16[4,128,64]{1,...) while((s32[]{:T(128)}, f32[4,128,64]{1,2,0:T(8,128)S(1)}, ...), condition=%wide.region_7.8_spmd.clone, body=%wide.region_6.7_spmd.sunk.clone | while | flops 271581184 | bytes 8589409 | solution.py:207
  483.1 4.0 fusion.61
  488.0 4.1 all-to-all-start.2
  492.2 13.1 %all-to-all-done.2 = bf16[8,128,384]{2,1,0:T(8,128)(2,1)S(1)} async-done(((bf16[8,128,384]{2,1,0:T(8,128)(2,1)}), bf16[8,128,384]{2,1,0:T(8,128)(2,1)S(1)}, u32[]{:S(2)}, u32[]{:S(2)}) %all-to-all-start.2) | async-done | bytes 786464 | tf_op jit(solution)/shard_map/all_to_all | solution.py:65
  506.5 7.6 %all_to_all.34 = f32[8,128,1]{1,2,0:T(1,128)S(1)} all-to-all(f32[8,128,1]{1,2,0:T(1,128)S(1)} %broadcast_in_dim.62), channel_id=1, replica_groups=mesh['grp'=2,'seq_0'=2,'seq_1'=16,'head_0'=4,'head_1'=2] {'head_0','head..., dimensions={0} | all-to-all | bytes 8192 | tf_op jit(solution)/shard_map/all_to_all | solution.py:35
  515.5 24.9 %all_to_all.35 = f32[64,1,384]{2,1,0:T(1,128)S(1)} all-to-all(f32[64,1,384]{2,1,0:T(1,128)S(1)} %copy.84), channel_id=1, replica_groups=mesh['grp'=2,'seq_0'=2,'seq_1'=16,'head_0'=4,'head_1'=2] {'grp','seq_0',..., dimensions={0} | all-to-all | bytes 196608 | tf_op jit(solution)/shard_map/all_to_all | solution.py:76
  541.2 6.0 %all-to-all-start.5 = ((f32[64,1,384]{2,1,0:T(1,128)}), f32[64,1,384]{2,1,0:T(1,128)S(1)}, u32[]{:S(2)}, u32[]{:S(2)}) async-start(f32[64,1,384]{2,1,0:T(1,128)} %broadcast_in_dim.63), calls=%async_computation.5 | async-start | bytes 196608 | tf_op jit(solution)/shard_map/all_to_all | solution.py:35
  547.9 13.5 %all-to-all-done.5 = f32[64,1,384]{2,1,0:T(1,128)S(1)} async-done(((f32[64,1,384]{2,1,0:T(1,128)}), f32[64,1,384]{2,1,0:T(1,128)S(1)}, u32[]{:S(2)}, u32[]{:S(2)}) %all-to-all-start.5) | async-done | bytes 98336 | tf_op jit(solution)/shard_map/all_to_all | solution.py:35
  (156 shorter events, 79.1 us)
Async XLA Ops:
  7.2 94.2 %copy-start = (bf16[64,3072]{1,0:T(8,128)(2,1)S(1)}, bf16[64,3072]{1,0:T(8,128)(2,1)}, u32[]{:S(2)}) copy-start(bf16[64,3072]{1,0:T(8,128)(2,1)} %param.16) | copy-start | bytes 1179652
  7.2 25.0 %copy-start.2 = (bf16[1,1,2,32,512]{4,3,2,1,0:T(8,128)(2,1)S(1)}, bf16[1,1,2,32,512]{4,3,2,1,0:T(8,128)(2,1)}, u32[]{:S(2)}) copy-start(bf16[1,1,2,32,512]{4,3,2,1,0:T(8,128)(2,1)} %param.12) | copy-start | bytes 196612
  7.2 159.0 %all-gather.4.cloned.1.call-start = ((), (), s32[]{:S(2)}) async-start(), calls=%async_computation.6 | async-start | bytes 4866048 | tf_op jit(solution)/shard_map/all_gather | solution.py:181
  7.2 14.4 %collective-permute-start = (bf16[1,2,32,512]{3,2,1,0:T(8,128)(2,1)}, bf16[1,2,32,512]{3,2,1,0:T(8,128)(2,1)S(1)}, u32[]{:S(2)}, u32[]{:S(2)}) collective-permute-start(bf16[1,2,32,512]{3,2,1,0:T(8,128)(2,1)} %bitcast.368), channel_id=1, source_target_pairs={{0,16},{8,24},{16,32},{24,40},{32,48},{40,56},{48,64},{56,72},{64,... | collective-permute-start | bytes 196616 | tf_op jit(solution)/shard_map/ppermute | solution.py:17
  12.6 11.3 %collective-permute-start.1 = (bf16[1,2,32,512]{3,2,1,0:T(8,128)(2,1)}, bf16[1,2,32,512]{3,2,1,0:T(8,128)(2,1)S(1)}, u32[]{:S(2)}, u32[]{:S(2)}) collective-permute-start(bf16[1,2,32,512]{3,2,1,0:T(8,128)(2,1)} %bitcast.369), channel_id=1, source_target_pairs={{0,8},{8,16},{16,24},{24,32},{32,40},{40,48},{48,56},{56,64},{64,7... | collective-permute-start | bytes 196616 | tf_op jit(solution)/shard_map/ppermute | solution.py:17
  24.7 3.0 collective-permute-start.2
  26.3 6.2 %copy-start.3 = (bf16[3,3,3,512,16]{3,4,2,1,0:T(8,128)(2,1)S(1)}, bf16[3,3,3,512,16]{3,4,2,1,0:T(8,128)(2,1)}, u32[]{:S(2)}) copy-start(bf16[3,3,3,512,16]{3,4,2,1,0:T(8,128)(2,1)} %param.13) | copy-start | bytes 1327108
  26.3 4.9 collective-permute-start.3
  28.5 5.0 copy-start.6
  61.5 10.2 %copy-start.7 = (s32[128]{0:T(128)S(1)}, s32[128]{0:T(128)}, u32[]{:S(2)}) copy-start(s32[128]{0:T(128)} %param.15) | copy-start | bytes 1540
  64.2 17.8 %all-to-all-start.1 = ((bf16[8,2,16384]{2,1,0:T(2,128)(2,1)}), bf16[8,2,16384]{2,1,0:T(2,128)(2,1)S(1)}, u32[]{:S(2)}, u32[]{:S(2)}) async-start(bf16[8,2,16384]{2,1,0:T(2,128)(2,1)} %reshape.226), calls=%async_computation.1 | async-start | bytes 1048576 | tf_op jit(solution)/shard_map/all_to_all | solution.py:35
  71.6 243.1 %all-gather.6.cloned.1.call-start = ((), (), s32[]{:S(2)}) async-start(), calls=%async_computation.7 | async-start | bytes 4325376 | tf_op jit(solution)/shard_map/all_gather | solution.py:54
  102.1 70.9 %copy-start.1 = (f32[128,3072]{1,0:T(8,128)}, f32[128,3072]{1,0:T(8,128)S(1)}, u32[]{:S(2)}) copy-start(f32[128,3072]{1,0:T(8,128)S(1)} %broadcast_multiply_fusion) | copy-start | bytes 4718596
  102.1 70.9 %copy-start.5 = (f32[3072]{0:T(1024)S(1)}, f32[3072]{0:T(1024)}, u32[]{:S(2)}) copy-start(f32[3072]{0:T(1024)} %param.17) | copy-start | bytes 36868
  172.9 5.2 copy-start.4
  177.9 277.4 %all-gather.8.cloned.1.call-start = ((), (), s32[]{:S(2)}) async-start(), calls=%async_computation.8 | async-start | bytes 4325376 | tf_op jit(solution)/shard_map/all_gather | solution.py:54
  488.0 17.3 %all-to-all-start.2 = ((bf16[8,128,384]{2,1,0:T(8,128)(2,1)}), bf16[8,128,384]{2,1,0:T(8,128)(2,1)S(1)}, u32[]{:S(2)}, u32[]{:S(2)}) async-start(bf16[8,128,384]{2,1,0:T(8,128)(2,1)} %bitcast.294), calls=%async_computation.2 | async-start | bytes 1572864 | tf_op jit(solution)/shard_map/all_to_all | solution.py:65
  541.2 20.2 %all-to-all-start.5 = ((f32[64,1,384]{2,1,0:T(1,128)}), f32[64,1,384]{2,1,0:T(1,128)S(1)}, u32[]{:S(2)}, u32[]{:S(2)}) async-start(f32[64,1,384]{2,1,0:T(1,128)} %broadcast_in_dim.63), calls=%async_computation.5 | async-start | bytes 196608 | tf_op jit(solution)/shard_map/all_to_all | solution.py:35
Sparse Core Ops, SparseCore 0:
  26.4 139.7 all-gather.3
  178.0 136.6 all-gather.5
  316.7 138.4 all-gather.7
where the time goes:
time: 570 us; the launch traced here: 569 us
  waiting for transfers between devices  297 us (52%)
  blocking collectives  118 us (21%)
  matrix products  57.1 us (10%)
  local copies, waits for them, and re-layouts  44.1 us (8%)
  starting transfers between devices  30 us (5%)
  between operations  14.2 us (2%)
  other arithmetic  7.52 us (1%)
    all_gather x2, waiting for transfers between devices, side_by_side(): result = lax.all_gather(both, axis, axis=dim, tiled=True)  186 us
    all_gather x1, waiting for transfers between devices, per_device(): full_weight = lax.all_gather(qkv_weight, SEQ, axis=0, tiled=True)  64.1 us
    all_gather x1, blocking collectives, side_by_side(): result = lax.all_gather(both, axis, axis=dim, tiled=True)  61.5 us
    all_to_all x2, blocking collectives, from_everyone(): return lax.all_to_all(copies, axis, split_axis=0, concat_axis=0, tiled=True)  31.6 us
    all_to_all x1, blocking collectives, sent_and_summed_2(): lax.all_to_all(blocks, axis, split_axis=0, concat_axis=0, tiled=True)  24.9 us
    all_to_all x2, waiting for transfers between devices, from_everyone(): return lax.all_to_all(copies, axis, split_axis=0, concat_axis=0, tiled=True)  23.7 us
    reshape x2, local copies, waits for them, and re-layouts, patchify(): return blocks.reshape(frames * (rows // 2) * (columns // 2), 4 * channels)  17.6 us
    all_to_all x2, starting transfers between devices, from_everyone(): return lax.all_to_all(copies, axis, split_axis=0, concat_axis=0, tiled=True)  13.5 us
  transfers between devices with their start and end apart: 10, of which 9 were waited for; matrix products, arithmetic and copies ran while one was open for 10% of the time, Pallas kernels for 0%

commit v1 on v0

--- a/solution.py
+++ b/solution.py
@@ -178,7 +178,8 @@
     inverse = lax.rsqrt(jnp.mean(mixed * mixed, axis=-1, keepdims=True) + 1e-06)
     normal = mixed * inverse
     hidden = (normal * norm_gain).astype(jnp.bfloat16)
-    full_weight = lax.all_gather(qkv_weight, SEQ, axis=0, tiled=True)
+    sent = jnp.stack([qkv_weight] * lax.axis_size(SEQ))
+    full_weight = jnp.concatenate(lax.all_to_all(sent, SEQ, 0, 0), axis=0)
     local_width = full_weight.shape[2]
     head_local = local_width // HEAD_DIM
     flat_weight = full_weight.reshape(D, 3 * local_width)

time: 570 us -> 717 us (1.26)
  waiting for transfers between devices: 297 us -> 412 us
  blocking collectives: 118 us -> 136 us
  local copies, waits for them, and re-layouts: 44.1 us -> 60.6 us
    all_to_all x0 -> x1, waiting for transfers between devices: none -> 185 us  [per_device(): full_weight = jnp.concatenate(lax.all_to_all(sent, SEQ, 0, 0), axis=0)]
    all_gather x1 -> x0, waiting for transfers between devices: 64.1 us -> none  [per_device(): full_weight = lax.all_gather(qkv_weight, SEQ, axis=0, tiled=True)]
    all_to_all x2 -> x3, blocking collectives: 31.6 us -> 48.6 us  [from_everyone(): return lax.all_to_all(copies, axis, split_axis=0, concat_axis=0, tiled=True)]
    another operation x3 -> x2, local copies, waits for them, and re-layouts: 0.32 us -> 15.7 us  [the longest x1 12.1 us: per_device(): flat_weight = full_weight.reshape(D, 3 * local_width)]
    all_to_all x2 -> x1, waiting for transfers between devices: 23.7 us -> 13.5 us  [from_everyone(): return lax.all_to_all(copies, axis, split_axis=0, concat_axis=0, tiled=True)]
    all_to_all x0 -> x1, local copies, waits for them, and re-layouts: none -> 8.37 us  [per_device(): full_weight = jnp.concatenate(lax.all_to_all(sent, SEQ, 0, 0), axis=0)]
    all_to_all x2 -> x1, starting transfers between devices: 13.5 us -> 6.01 us  [from_everyone(): return lax.all_to_all(copies, axis, split_axis=0, concat_axis=0, tiled=True)]
  transfers between devices with their start and end apart: 10 -> 9, of which waited for: 9 -> 8; matrix products, arithmetic and copies ran while one was open for 10% -> 7% of each run, Pallas kernels for 0% -> 0%
where the time goes in v1:
time: 717 us; the launch traced here: 715 us
  waiting for transfers between devices  412 us (57%)
  blocking collectives  136 us (19%)
  local copies, waits for them, and re-layouts  60.6 us (8%)
  matrix products  56.3 us (8%)
  starting transfers between devices  29.4 us (4%)
  between operations  14.5 us (2%)
    all_gather x2, waiting for transfers between devices, side_by_side(): result = lax.all_gather(both, axis, axis=dim, tiled=True)  189 us
    all_to_all x1, waiting for transfers between devices, per_device(): full_weight = jnp.concatenate(lax.all_to_all(sent, SEQ, 0, 0), axis=0)  185 us
    all_gather x1, blocking collectives, side_by_side(): result = lax.all_gather(both, axis, axis=dim, tiled=True)  61.7 us
    all_to_all x3, blocking collectives, from_everyone(): return lax.all_to_all(copies, axis, split_axis=0, concat_axis=0, tiled=True)  48.6 us
    all_to_all x1, blocking collectives, sent_and_summed_2(): lax.all_to_all(blocks, axis, split_axis=0, concat_axis=0, tiled=True)  25.2 us
    reshape x2, local copies, waits for them, and re-layouts, patchify(): return blocks.reshape(frames * (rows // 2) * (columns // 2), 4 * channels)  17.6 us
  transfers between devices with their start and end apart: 9, of which 8 were waited for; matrix products, arithmetic and copies ran while one was open for 7% of the time, Pallas kernels for 0%

profile of v1, /device:TPU:2, one launch (start us, length us, event | category | flops | bytes accessed | tf_op | source)
XLA Modules:
  0.0 715.0 jit_solution(4141928763236695548)
XLA Ops:
  7.2 5.3 collective-permute-start
  16.3 5.2 collective-permute-done
  36.4 24.1 %all_to_all.38 = bf16[32,2,512]{2,1,0:T(2,128)(2,1)S(1)} all-to-all(bf16[32,2,512]{2,1,0:T(2,128)(2,1)S(1)} %reshape.227), channel_id=1, replica_groups=mesh['grp'=2,'seq_0'=2,'seq_1'=16,'head_0'=4,'head_1'=2] {'seq_0','seq_1'}, dimensions={0} | all-to-all | bytes 131072 | tf_op jit(solution)/shard_map/all_to_all | solution.py:35
  63.5 16.9 %all_to_all.39 = bf16[8,2,16384]{2,1,0:T(2,128)(2,1)S(1)} all-to-all(bf16[8,2,16384]{2,1,0:T(2,128)(2,1)S(1)} %reshape.229), channel_id=1, replica_groups=mesh['grp'=2,'seq_0'=2,'seq_1'=16,'head_0'=4,'head_1'=2] {'head_0','head..., dimensions={0} | all-to-all | bytes 1048576 | tf_op jit(solution)/shard_map/all_to_all | solution.py:35
  84.1 6.3 all-to-all-start.2
  91.7 9.6 %copy.75 = bf16[32,8,16,2,2,16]{5,4,3,2,1,0:T(2,128)(2,1)} copy(bf16[32,8,16,2,2,16]{0,5,4,2,3,1:T(8,128)(2,1)S(1)} %bitcast.364) | data formatting | bytes 1048576 | tf_op jit(solution)/shard_map/reshape | solution.py:102
  101.4 8.0 %reshape.226 = bf16[4096,64]{1,0:T(8,128)(2,1)S(1)} reshape(bf16[32,8,16,2,2,16]{5,4,3,2,1,0:T(2,128)(2,1)} %copy.75) | data formatting | bytes 1048576 | tf_op jit(solution)/shard_map/reshape | solution.py:102
  110.8 185.3 %all-to-all-done.2 = bf16[32,96,3,256]{3,1,2,0:T(8,128)(2,1)} async-done(((bf16[32,96,3,256]{3,1,2,0:T(8,128)(2,1)}), bf16[32,96,3,256]{3,1,2,0:T(8,128)(2,1)}, u32[]{:S(2)}, u32[]{:S(2)}) %all-to-all-start.2) | async-done | bytes 4718624 | tf_op jit(solution)/shard_map/all_to_all | solution.py:182
  296.1 8.4 %copy.59 = bf16[32,96,3,256]{1,0,3,2:T(8,128)(2,1)} copy(bf16[32,96,3,256]{3,1,2,0:T(8,128)(2,1)} %all-to-all-done.2) | data formatting | bytes 9437184 | tf_op jit(solution)/shard_map/all_to_all | solution.py:182
  304.4 12.1 %reshape_reshape.6 = bf16[3072,768]{0,1:T(8,128)(2,1)} reshape(bf16[32,96,3,256]{1,0,3,2:T(8,128)(2,1)} %copy.59) | data formatting | bytes 9437184 | tf_op jit(solution)/shard_map/reshape;reshape | solution.py:185
  316.6 4.0 convolution_convert_fusion.2
  322.4 138.6 %all-gather.3.cloned.1.call-done = bf16[4096,512]{0,1:T(8,128)(2,1)} async-done(((bf16[128,512]{0,1:T(8,128)(2,1)}), bf16[4096,512]{0,1:T(8,128)(2,1)}) %all-gather.3.cloned.1.call-update) | async-done | bytes 4194320 | tf_op jit(solution)/shard_map/all_gather | solution.py:54
  461.0 4.7 fusion.153
  465.7 23.7 %while.30 = (s32[]{:T(128)}, bf16[4,128,64]{1,2,0:T(8,128)(2,1)S(1)}, f32[4,128]{1,0:T(4,128)S(1)}, f32[4,128]{1,0:T(4,128)S(1)}, bf16[4,128,64]{1,2,0:T(8,128)(...) while((s32[]{:T(128)}, ...), condition=%wide.region_5.6_spmd.clone, body=%wide.region_1.0_spmd.sunk.clone | while | flops 273727232 | bytes 10628201 | solution.py:191
  489.4 61.7 %all_gather.11 = f32[4096,8]{0,1:T(8,128)S(1)} all-gather(f32[128,8]{0,1:T(8,128)S(1)} %pad_maximum_fusion.14), channel_id=1, replica_groups=mesh['grp'=2,'seq_0'=2,'seq_1'=16,'head_0'=4,'head_1'=2] {'seq_0','seq_1'}, dimensions={0}, use_global_device_ids=true | all-gather | bytes 135168 | tf_op jit(solution)/shard_map/all_gather | solution.py:54
  551.2 50.3 %all-gather.5.cloned.1.call-done = bf16[4096,512]{0,1:T(8,128)(2,1)} async-done(((bf16[128,512]{0,1:T(8,128)(2,1)}), bf16[4096,512]{0,1:T(8,128)(2,1)}) %all-gather.5.cloned.1.call-update) | async-done | bytes 4194320 | tf_op jit(solution)/shard_map/all_gather | solution.py:54
  601.5 4.8 fusion.152
  606.2 22.7 %while.31 = (s32[]{:T(128)}, f32[4,128,64]{1,2,0:T(8,128)S(1)}, bf16[4,128,64]{1,2,0:T(8,128)(2,1)S(1)}, bf16[4,4096,64]{1,2,0:T(8,128)(2,1)}, bf16[4,128,64]{1,...) while((s32[]{:T(128)}, f32[4,128,64]{1,2,0:T(8,128)S(1)}, ...), condition=%wide.region_7.8_spmd.clone, body=%wide.region_6.7_spmd.sunk.clone | while | flops 271581184 | bytes 8589409 | solution.py:208
  633.1 4.8 all-to-all-start.3
  638.0 13.1 %all-to-all-done.3 = bf16[8,128,384]{2,1,0:T(8,128)(2,1)S(1)} async-done(((bf16[8,128,384]{2,1,0:T(8,128)(2,1)}), bf16[8,128,384]{2,1,0:T(8,128)(2,1)S(1)}, u32[]{:S(2)}, u32[]{:S(2)}) %all-to-all-start.3) | async-done | bytes 786464 | tf_op jit(solution)/shard_map/all_to_all | solution.py:65
  652.2 7.6 %all_to_all.40 = f32[8,128,1]{1,2,0:T(1,128)S(1)} all-to-all(f32[8,128,1]{1,2,0:T(1,128)S(1)} %broadcast_in_dim.62), channel_id=1, replica_groups=mesh['grp'=2,'seq_0'=2,'seq_1'=16,'head_0'=4,'head_1'=2] {'head_0','head..., dimensions={0} | all-to-all | bytes 8192 | tf_op jit(solution)/shard_map/all_to_all | solution.py:35
  661.2 25.2 %all_to_all.41 = f32[64,1,384]{2,1,0:T(1,128)S(1)} all-to-all(f32[64,1,384]{2,1,0:T(1,128)S(1)} %copy.73), channel_id=1, replica_groups=mesh['grp'=2,'seq_0'=2,'seq_1'=16,'head_0'=4,'head_1'=2] {'grp','seq_0',..., dimensions={0} | all-to-all | bytes 196608 | tf_op jit(solution)/shard_map/all_to_all | solution.py:76
  687.3 6.0 all-to-all-start.6
  694.0 13.5 %all-to-all-done.6 = f32[64,1,384]{2,1,0:T(1,128)S(1)} async-done(((f32[64,1,384]{2,1,0:T(1,128)}), f32[64,1,384]{2,1,0:T(1,128)S(1)}, u32[]{:S(2)}, u32[]{:S(2)}) %all-to-all-start.6) | async-done | bytes 98336 | tf_op jit(solution)/shard_map/all_to_all | solution.py:35
  (154 shorter events, 84.8 us)
Async XLA Ops:
  7.2 102.9 %copy-start = (bf16[64,3072]{1,0:T(8,128)(2,1)S(1)}, bf16[64,3072]{1,0:T(8,128)(2,1)}, u32[]{:S(2)}) copy-start(bf16[64,3072]{1,0:T(8,128)(2,1)} %param.16) | copy-start | bytes 1179652
  7.2 25.1 %copy-start.3 = (bf16[3,3,3,512,16]{3,4,2,1,0:T(8,128)(2,1)S(1)}, bf16[3,3,3,512,16]{3,4,2,1,0:T(8,128)(2,1)}, u32[]{:S(2)}) copy-start(bf16[3,3,3,512,16]{3,4,2,1,0:T(8,128)(2,1)} %param.13) | copy-start | bytes 1327108
  7.2 14.4 %collective-permute-start = (bf16[1,2,32,512]{3,2,1,0:T(8,128)(2,1)}, bf16[1,2,32,512]{3,2,1,0:T(8,128)(2,1)S(1)}, u32[]{:S(2)}, u32[]{:S(2)}) collective-permute-start(bf16[1,2,32,512]{3,2,1,0:T(8,128)(2,1)} %bitcast.368), channel_id=1, source_target_pairs={{0,16},{8,24},{16,32},{24,40},{32,48},{40,56},{48,64},{56,72},{64,... | collective-permute-start | bytes 196616 | tf_op jit(solution)/shard_map/ppermute | solution.py:17
  12.5 11.3 %collective-permute-start.1 = (bf16[1,2,32,512]{3,2,1,0:T(8,128)(2,1)}, bf16[1,2,32,512]{3,2,1,0:T(8,128)(2,1)S(1)}, u32[]{:S(2)}, u32[]{:S(2)}) collective-permute-start(bf16[1,2,32,512]{3,2,1,0:T(8,128)(2,1)} %bitcast.369), channel_id=1, source_target_pairs={{0,8},{8,16},{16,24},{24,32},{32,40},{40,48},{48,56},{56,64},{64,7... | collective-permute-start | bytes 196616 | tf_op jit(solution)/shard_map/ppermute | solution.py:17
  24.7 8.7 %copy-start.6 = (f32[16]{0:T(128)S(1)}, f32[16]{0:T(128)}, u32[]{:S(2)}) copy-start(f32[16]{0:T(128)} %param.14) | copy-start | bytes 196
  24.7 8.8 %copy-start.2 = (bf16[1,1,2,32,512]{4,3,2,1,0:T(8,128)(2,1)S(1)}, bf16[1,1,2,32,512]{4,3,2,1,0:T(8,128)(2,1)}, u32[]{:S(2)}) copy-start(bf16[1,1,2,32,512]{4,3,2,1,0:T(8,128)(2,1)} %param.12) | copy-start | bytes 196612
  24.7 2.9 collective-permute-start.2
  26.4 4.8 collective-permute-start.3
  84.1 6.6 copy-start.7
  84.1 212.0 %all-to-all-start.2 = ((bf16[32,96,3,256]{3,1,2,0:T(8,128)(2,1)}), bf16[32,96,3,256]{3,1,2,0:T(8,128)(2,1)}, u32[]{:S(2)}, u32[]{:S(2)}) async-start(bf16[32,96,3,256]{3,1,2,0:T(8,128)(2,1)} %stack.5), calls=%async_computation.2 | async-start | bytes 9437184 | tf_op jit(solution)/shard_map/all_to_all | solution.py:182
  90.4 370.6 %all-gather.3.cloned.1.call-start = ((), (), s32[]{:S(2)}) async-start(), calls=%async_computation.7 | async-start | bytes 4325376 | tf_op jit(solution)/shard_map/all_gather | solution.py:54
  110.8 205.7 %copy-start.1 = (f32[128,3072]{1,0:T(8,128)}, f32[128,3072]{1,0:T(8,128)S(1)}, u32[]{:S(2)}) copy-start(f32[128,3072]{1,0:T(8,128)S(1)} %broadcast_multiply_fusion) | copy-start | bytes 4718596
  304.4 12.1 %copy-start.5 = (f32[3072]{0:T(1024)S(1)}, f32[3072]{0:T(1024)}, u32[]{:S(2)}) copy-start(f32[3072]{0:T(1024)} %param.17) | copy-start | bytes 36868
  316.5 5.0 copy-start.4
  321.5 280.0 %all-gather.5.cloned.1.call-start = ((), (), s32[]{:S(2)}) async-start(), calls=%async_computation.8 | async-start | bytes 4325376 | tf_op jit(solution)/shard_map/all_gather | solution.py:54
  633.1 17.9 %all-to-all-start.3 = ((bf16[8,128,384]{2,1,0:T(8,128)(2,1)}), bf16[8,128,384]{2,1,0:T(8,128)(2,1)S(1)}, u32[]{:S(2)}, u32[]{:S(2)}) async-start(bf16[8,128,384]{2,1,0:T(8,128)(2,1)} %bitcast.295), calls=%async_computation.3 | async-start | bytes 1572864 | tf_op jit(solution)/shard_map/all_to_all | solution.py:65
  687.3 20.2 %all-to-all-start.6 = ((f32[64,1,384]{2,1,0:T(1,128)}), f32[64,1,384]{2,1,0:T(1,128)S(1)}, u32[]{:S(2)}, u32[]{:S(2)}) async-start(f32[64,1,384]{2,1,0:T(1,128)} %broadcast_in_dim.63), calls=%async_computation.6 | async-start | bytes 196608 | tf_op jit(solution)/shard_map/all_to_all | solution.py:35
Sparse Core Ops, SparseCore 0:
  321.6 139.3 all-gather.2
  463.0 138.4 all-gather.4
